TPU v7x, 32 devices: a whole 2x2x4 slice. The times are simulated.
32 devices in a mesh: dom: 1, blk: 4 (over z), grp: 8 (over y, x, core), sub: 1.
Axes of the slice: x: 2, y: 2, z: 4, core: 2. Of those that a mesh axis runs over, the one named last changes fastest.
Arguments:
- records: bfloat16 [512, 8, 1024], P(('dom', 'blk', 'grp')), may hold values from -40 to 40
- flags: int32 [512, 8], P(('dom', 'blk', 'grp')), may hold values 0 or 1
Outputs:
- correlations: bfloat16 [256, 512, 3, 128], P('sub', ('dom', 'blk', 'grp'))
All inputs are finite; a program needn't handle non-finite values. No bound on the sum of `flags` on one device may be relied on, other than what follows from the above.
Results may differ from a plain program's by a relative error of at most 0.012.
Values may be sent and summed in bfloat16 or wider, within the bound.
A program may use at most 64 MiB of HBM per device.

v0:
```python
import math

import jax
import jax.numpy as jnp
from jax import lax
from jax.sharding import PartitionSpec as P

LAGS = 256
STEPS = 3


def shifted(value, axis, steps):
    count = lax.axis_size(axis)
    pairs = [(source, (source + steps) % count) for source in range(count)]
    return lax.ppermute(value, axis, pairs)


def on_device(records, flags):
    channels, segs, length = records.shape
    bins = length // 2
    splits = lax.axis_size("sub")
    half = bins // splits
    first_bin = lax.axis_index("sub") * half
    freq = first_bin + jnp.arange(half, dtype=jnp.int32)
    samples = jnp.arange(length, dtype=jnp.int32)
    phase = jnp.mod(samples[:, None] * freq[None, :], length).astype(jnp.float32)
    angle = 2.0 * math.pi * phase / length
    transform = jnp.concatenate([jnp.cos(angle), -jnp.sin(angle)], axis=1)
    spectra = jnp.dot(
        records.astype(jnp.float32).reshape(channels * segs, length),
        transform,
        precision=lax.Precision.HIGH,
    )
    real_part = spectra[:, :half]
    imag_part = spectra[:, half:]
    power = real_part * real_part + imag_part * imag_part
    band = lax.psum(jnp.sum(power, axis=1).reshape(channels, segs), "sub")
    level = (band / bins).reshape(channels * segs, 1)
    valid = flags.astype(jnp.float32).reshape(channels * segs, 1)
    scale = valid / jnp.sqrt(power + level + 1e-06)
    white = jnp.stack(
        [
            (real_part * scale).reshape(channels, segs, half),
            (imag_part * scale).reshape(channels, segs, half),
        ],
        axis=1,
    ).astype(jnp.bfloat16)
    own_flags = flags.astype(jnp.bfloat16)
    stacked = jnp.stack(
        [
            white.reshape(channels, 2 * segs, half),
            jnp.concatenate([white[:, 1], -white[:, 0]], axis=1),
        ]
    )
    offset = jnp.arange(LAGS, dtype=jnp.int32) - LAGS // 2
    lag_phase = jnp.mod(freq[:, None] * offset[None, :], length).astype(jnp.float32)
    lag_angle = 2.0 * math.pi * lag_phase / length
    lag_table = jnp.stack([jnp.cos(lag_angle), -jnp.sin(lag_angle)]).astype(jnp.bfloat16)
    keep_rows = LAGS // splits
    block = (
        lax.all_gather(white, "grp", axis=0, tiled=True),
        lax.all_gather(own_flags, "grp", axis=0, tiled=True),
    )
    moving = block
    results = []
    for step in range(STEPS):
        if step == 0:
            partner = block
        else:
            source = moving
            distance = 1
            moving = shifted((source[0], source[1]), "blk", distance)
            partner = moving
        other, other_flags = partner
        width = other.shape[0]
        cross = jnp.einsum(
            "cisf,jsf->cijf",
            stacked,
            other.reshape(width, 2 * segs, half),
            preferred_element_type=jnp.float32,
        ).astype(jnp.bfloat16)
        count = jnp.dot(own_flags, other_flags.T, preferred_element_type=jnp.float32)

        def lag_terms(start, rows, cross=cross):
            return jnp.einsum("cfl,cijf->lij", lag_table, cross, preferred_element_type=jnp.float32)

        summed = lax.psum_scatter(
            lag_terms(jnp.int32(0), keep_rows * lax.axis_size("sub")).astype(jnp.bfloat16),
            "sub",
            scatter_dimension=0,
            tiled=True,
        ).astype(jnp.float32)
        norm = jnp.sqrt(bins * jnp.maximum(count, 1.0))
        results.append((summed / norm[None]).astype(jnp.bfloat16))
    return jnp.stack(results, axis=2)


def solution(mesh):
    return jax.shard_map(
        on_device,
        mesh=mesh,
        in_specs=(P(("dom", "blk", "grp"), None, None), P(("dom", "blk", "grp"), None)),
        out_specs=P("sub", ("dom", "blk", "grp"), None, None),
        check_vma=False,
    )
```

profile of v0, /device:TPU:0, one launch (start us, length us, event | category | flops | bytes accessed | tf_op | source)
XLA Modules:
  0.0 175.8 jit_solution(3370337687247140822)
XLA Ops:
  6.5 8.2 %sine_negate_fusion = (f32[1024,512]{1,0:T(8,128)S(1)}, f32[1024,512]{1,0:T(8,128)S(1)}) fusion(), kind=kLoop, calls=%fused_computation.26 | loop fusion | flops 7864320 | bytes 4194304 | tf_op jit(solution)/shard_map/neg | solution.py:28
  14.8 0.9 fusion.22
  16.2 0.7 maximum_convert_fusion
  16.9 30.7 %all-gather.3.cloned.1.call-done = bf16[128,2,8,512]{3,2,1,0:T(8,128)(2,1)} async-done(((bf16[16,2,8,512]{3,2,1,0:T(8,128)(2,1)}), bf16[128,2,8,512]{3,2,1,0:T(8,128)(2,1)}) %all-gather.3.cloned.1.call-update) | async-done | bytes 2097168 | tf_op jit(solution)/shard_map/all_gather | solution.py:61
  47.7 1.5 collective-permute-start
  49.2 8.8 %all-gather = bf16[8,16,8]{1,2,0:T(8,128)(2,1)S(1)} all-gather(bf16[1,16,8]{1,2,0:T(8,128)(2,1)S(1)} %bitcast.82), channel_id=1, replica_groups=mesh['dom'=1,'blk'=4,'grp'=8,'sub'=1] {'grp'}, dimensions={0}, use_global_device_ids=true | all-gather | bytes 2304 | tf_op jit(solution)/shard_map/all_gather | solution.py:62
  58.1 1.7 collective-permute-start.1
  59.8 1.0 slice_bitcast_fusion
  61.0 3.2 %cosine_convert_fusion = (bf16[1,512,256]{1,2,0:T(8,128)(2,1)}, bf16[1,512,256]{1,2,0:T(8,128)(2,1)}) fusion(s32[256]{0:T(256)S(1)} %iota_add_fusion), kind=kLoop, calls=%fused_computation.54 | loop fusion | flops 2228224 | bytes 525312 | tf_op jit(solution)/shard_map/convert
  64.3 6.5 %copy.29 = bf16[2,16,16,512]{2,1,0,3:T(8,128)(2,1)} copy(bf16[2,16,16,512]{3,2,1,0:T(8,128)(2,1)S(1)} %pad_maximum_fusion.1) | data formatting | bytes 1048576 | tf_op jit(solution)/shard_map/stack | solution.py:49
  70.7 26.9 %collective-permute-done.1 = bf16[128,8]{0,1:T(8,128)(2,1)S(1)} collective-permute-done((bf16[128,8]{0,1:T(8,128)(2,1)S(1)}, bf16[128,8]{0,1:T(8,128)(2,1)S(1)}, u32[]{:S(2)}, u32[]{:S(2)}) %collective-permute-start.1) | collective-permute-done | bytes 2080 | tf_op jit(solution)/shard_map/ppermute | solution.py:15
  97.8 5.2 %collective-permute-done.3 = bf16[128,8]{0,1:T(8,128)(2,1)S(1)} collective-permute-done((bf16[128,8]{0,1:T(8,128)(2,1)S(1)}, bf16[128,8]{0,1:T(8,128)(2,1)S(1)}, u32[]{:S(2)}, u32[]{:S(2)}) %collective-permute-start.3) | collective-permute-done | bytes 2080 | tf_op jit(solution)/shard_map/ppermute | solution.py:15
  103.2 4.2 %copy.39 = bf16[128,16,512,1]{0,1,3,2:T(8,128)(2,1)S(1)} copy(bf16[128,16,512,1]{2,1,0,3:T(8,128)(2,1)} %bitcast.81) | data formatting | bytes 4194304 | tf_op jit(solution)/shard_map/reshape | solution.py:79
  107.6 3.5 %convert_bitcast_fusion.2 = bf16[2,16,128,512]{2,1,0,3:T(8,128)(2,1)S(1)} fusion(bf16[128,16,512,1]{0,1,3,2:T(8,128)(2,1)S(1)} %copy.39, bf16[2,16,16,512]{2,1,0,3:T(8,128)(2,1)} %copy.29), kind=kOutput, calls=%fused_computation.12 | convolution fusion | flops 69206016 | bytes 6815744 | tf_op jit(solution)/shard_map/cisf,jsf->cijf/dot_general | solution.py:76
  111.0 1.6 fusion.31
  112.6 4.2 %copy.41 = bf16[128,16,512,1]{0,1,3,2:T(8,128)(2,1)S(1)} copy(bf16[128,16,512,1]{2,1,0,3:T(8,128)(2,1)} %bitcast.19) | data formatting | bytes 4194304 | tf_op jit(solution)/shard_map/reshape | solution.py:79
  116.9 3.5 %convert_bitcast_fusion.1 = bf16[2,16,128,512]{2,1,0,3:T(8,128)(2,1)S(1)} fusion(bf16[128,16,512,1]{0,1,3,2:T(8,128)(2,1)S(1)} %copy.41, bf16[2,16,16,512]{2,1,0,3:T(8,128)(2,1)} %copy.29), kind=kOutput, calls=%fused_computation.11 | convolution fusion | flops 69206016 | bytes 6815744 | tf_op jit(solution)/shard_map/cisf,jsf->cijf/dot_general | solution.py:76
  120.4 2.6 %fusion.32 = bf16[256,16,1,128]{3,0,1,2:T(8,128)(2,1)} fusion(f32[16,128]{1,0:T(8,128)S(1)} %fusion.28, bf16[2,16,128,512]{2,1,0,3:T(8,128)(2,1)S(1)} %convert_bitcast_fusion.1, bf16[1,512,256]{1,2,0:T(8,128)(2,1)S(1)} %copy-done.6, bf16[1,512,256]{1,2,0:T(8,128)(2,1)S(1)} %copy-done.3), kind=kOutput, calls=%fused_computation.41 | convolution fusion | flops 1076887552 | bytes 5775360 | tf_op jit(solution)/shard_map/cfl,cijf->lij/dot_general | solution.py:85
  123.0 32.6 %collective-permute-done.2 = bf16[128,2,8,512]{3,2,1,0:T(8,128)(2,1)} collective-permute-done((bf16[128,2,8,512]{3,2,1,0:T(8,128)(2,1)}, bf16[128,2,8,512]{3,2,1,0:T(8,128)(2,1)}, u32[]{:S(2)}, u32[]{:S(2)}) %collective-permute-start.2) | collective-permute-done | bytes 2097184 | tf_op jit(solution)/shard_map/ppermute | solution.py:15
  155.5 4.2 %copy.43 = bf16[128,16,512,1]{0,1,3,2:T(8,128)(2,1)S(1)} copy(bf16[128,16,512,1]{2,1,0,3:T(8,128)(2,1)} %bitcast.25) | data formatting | bytes 4194304 | tf_op jit(solution)/shard_map/reshape | solution.py:79
  159.8 3.5 %convert_bitcast_fusion = bf16[2,16,128,512]{2,1,0,3:T(8,128)(2,1)S(1)} fusion(bf16[128,16,512,1]{0,1,3,2:T(8,128)(2,1)S(1)} %copy.43, bf16[2,16,16,512]{2,1,0,3:T(8,128)(2,1)} %copy.29), kind=kOutput, calls=%fused_computation.10 | convolution fusion | flops 69206016 | bytes 6815744 | tf_op jit(solution)/shard_map/cisf,jsf->cijf/dot_general | solution.py:76
  163.3 1.6 fusion.33
  164.9 0.3 pad_maximum_fusion
  165.2 3.7 %copy.38 = bf16[256,16,3,128]{3,1,2,0:T(8,128)(2,1)} copy(bf16[256,16,3,128]{3,0,1,2:T(8,128)(2,1)S(1)} %pad_maximum_fusion) | data formatting | bytes 6291456 | tf_op jit(solution)/shard_map/stack | solution.py:95
  (38 shorter events, 1.3 us)
Async XLA Ops:
  6.5 8.2 %copy-start = (bf16[16,8,1024]{2,1,0:T(8,128)(2,1)S(1)}, bf16[16,8,1024]{2,1,0:T(8,128)(2,1)}, u32[]{:S(2)}) copy-start(bf16[16,8,1024]{2,1,0:T(8,128)(2,1)} %param.2) | copy-start | bytes 786436
  6.5 41.2 %all-gather.3.cloned.1.call-start = ((), (), s32[]{:S(2)}) async-start(), calls=%async_computation | async-start | bytes 2359296 | tf_op jit(solution)/shard_map/all_gather | solution.py:61
  14.8 1.1 copy-start.8
  47.7 59.8 %collective-permute-start = (bf16[128,2,8,512]{3,2,1,0:T(8,128)(2,1)}, bf16[128,2,8,512]{3,2,1,0:T(8,128)(2,1)}, u32[]{:S(2)}, u32[]{:S(2)}) collective-permute-start(bf16[128,2,8,512]{3,2,1,0:T(8,128)(2,1)} %all-gather.3.cloned.1.call-done), channel_id=1, source_target_pairs={{0,8},{8,16},{16,24},{24,0},{1,9},{9,17},{17,25},{25,1},{2,10},{10... | collective-permute-start | bytes 6291464 | tf_op jit(solution)/shard_map/ppermute | solution.py:15
  58.1 39.5 %collective-permute-start.1 = (bf16[128,8]{0,1:T(8,128)(2,1)S(1)}, bf16[128,8]{0,1:T(8,128)(2,1)S(1)}, u32[]{:S(2)}, u32[]{:S(2)}) collective-permute-start(bf16[128,8]{0,1:T(8,128)(2,1)S(1)} %reshape.155), channel_id=1, source_target_pairs={{0,8},{8,16},{16,24},{24,0},{1,9},{9,17},{17,25},{25,1},{2,10},{10... | collective-permute-start | bytes 6152 | tf_op jit(solution)/shard_map/ppermute | solution.py:15
  97.6 5.4 %collective-permute-start.3 = (bf16[128,8]{0,1:T(8,128)(2,1)S(1)}, bf16[128,8]{0,1:T(8,128)(2,1)S(1)}, u32[]{:S(2)}, u32[]{:S(2)}) collective-permute-start(bf16[128,8]{0,1:T(8,128)(2,1)S(1)} %collective-permute-done.1), channel_id=1, source_target_pairs={{0,8},{8,16},{16,24},{24,0},{1,9},{9,17},{17,25},{25,1},{2,10},{10... | collective-permute-start | bytes 6152 | tf_op jit(solution)/shard_map/ppermute | solution.py:15
  107.5 3.6 %copy-start.2 = (bf16[1,512,256]{1,2,0:T(8,128)(2,1)S(1)}, bf16[1,512,256]{1,2,0:T(8,128)(2,1)}, u32[]{:S(2)}) copy-start(bf16[1,512,256]{1,2,0:T(8,128)(2,1)} %get-tuple-element.11) | copy-start | bytes 786436
  107.5 3.6 %copy-start.5 = (bf16[1,512,256]{1,2,0:T(8,128)(2,1)S(1)}, bf16[1,512,256]{1,2,0:T(8,128)(2,1)}, u32[]{:S(2)}) copy-start(bf16[1,512,256]{1,2,0:T(8,128)(2,1)} %get-tuple-element.12) | copy-start | bytes 786436
  107.5 48.0 %collective-permute-start.2 = (bf16[128,2,8,512]{3,2,1,0:T(8,128)(2,1)}, bf16[128,2,8,512]{3,2,1,0:T(8,128)(2,1)}, u32[]{:S(2)}, u32[]{:S(2)}) collective-permute-start(bf16[128,2,8,512]{3,2,1,0:T(8,128)(2,1)} %collective-permute-done), channel_id=1, source_target_pairs={{0,8},{8,16},{16,24},{24,0},{1,9},{9,17},{17,25},{25,1},{2,10},{10... | collective-permute-start | bytes 6291464 | tf_op jit(solution)/shard_map/ppermute | solution.py:15
  116.9 3.5 %copy-start.3 = (bf16[1,512,256]{1,2,0:T(8,128)(2,1)S(1)}, bf16[1,512,256]{1,2,0:T(8,128)(2,1)}, u32[]{:S(2)}) copy-start(bf16[1,512,256]{1,2,0:T(8,128)(2,1)} %get-tuple-element.11) | copy-start | bytes 786436
  116.9 3.5 %copy-start.6 = (bf16[1,512,256]{1,2,0:T(8,128)(2,1)S(1)}, bf16[1,512,256]{1,2,0:T(8,128)(2,1)}, u32[]{:S(2)}) copy-start(bf16[1,512,256]{1,2,0:T(8,128)(2,1)} %get-tuple-element.12) | copy-start | bytes 786436
  159.8 3.5 %copy-start.4 = (bf16[1,512,256]{1,2,0:T(8,128)(2,1)S(1)}, bf16[1,512,256]{1,2,0:T(8,128)(2,1)}, u32[]{:S(2)}) copy-start(bf16[1,512,256]{1,2,0:T(8,128)(2,1)} %get-tuple-element.11) | copy-start | bytes 786436
  159.8 3.5 %copy-start.7 = (bf16[1,512,256]{1,2,0:T(8,128)(2,1)S(1)}, bf16[1,512,256]{1,2,0:T(8,128)(2,1)}, u32[]{:S(2)}) copy-start(bf16[1,512,256]{1,2,0:T(8,128)(2,1)} %get-tuple-element.12) | copy-start | bytes 786436
  163.3 1.6 copy-start.1
Sparse Core Ops, SparseCore 0:
  17.1 30.5 all-gather.2
where the time goes:
time: 176 us
  waiting for transfers between devices  95.4 us (54%)
  local copies, waits for them, and re-layouts  23.2 us (13%)
  matrix products  17.6 us (10%)
  other arithmetic  13.9 us (8%)
  between operations  13.7 us (8%)
  blocking collectives  8.84 us (5%)
  starting transfers between devices  3.2 us (2%)
    ppermute x4, waiting for transfers between devices, shifted(): return lax.ppermute(value, axis, pairs)  64.6 us
    all_gather x1, waiting for transfers between devices, on_device(): lax.all_gather(white, 'grp', axis=0, tiled=True)  30.7 us
    reshape x3, local copies, waits for them, and re-layouts, on_device(): other.reshape(width, 2 * segs, half)  12.7 us
    dot_general x3, matrix products, on_device(): jnp.einsum('cisf,jsf->cijf', stacked, other.reshape(width, 2 * segs, half...  10.4 us
    all_gather x1, blocking collectives, on_device(): lax.all_gather(own_flags, 'grp', axis=0, tiled=True)  8.84 us
    neg x1, other arithmetic, on_device(): transform = jnp.concatenate([jnp.cos(angle), -jnp.sin(angle)], axis=1)  8.24 us
    another operation x1, local copies, waits for them, and re-layouts, on_device(): jnp.stack([white.reshape(channels, 2 * segs, half), jnp.concatenate([whit...  6.47 us
    dot_general x3, matrix products, lag_terms(): jnp.einsum('cfl,cijf->lij', lag_table, cross, preferred_element_type=jnp....  5.73 us
  transfers between devices with their start and end apart: 5, of which 4 were waited for; matrix products, arithmetic and copies ran while one was open for 18% of the time, Pallas kernels for 0%

commit v1 on v0

v1 whole, which is shorter than its diff:
```python
import functools

import jax
import jax.numpy as jnp
import ml_dtypes
import numpy as np
from jax import lax
from jax.experimental import pallas as pl
from jax.experimental.pallas import tpu as pltpu
from jax.sharding import PartitionSpec as P

LAGS = 256
STEPS = 3
LANES = 128
GROUP = 16
MESH = pl.DeviceIdType.MESH


def dft_tables(length):
    bins = length // 2
    phase = np.mod(np.arange(length)[:, None] * np.arange(bins)[None, :], length)
    angle = 2.0 * np.pi * phase / length
    return np.cos(angle).astype(np.float32), (-np.sin(angle)).astype(np.float32)


def lag_tables(length):
    bins = length // 2
    phase = np.mod((np.arange(LAGS) - LAGS // 2)[:, None] * np.arange(bins)[None, :], length)
    angle = 2.0 * np.pi * phase / length
    both = np.stack([np.cos(angle), -np.sin(angle)], axis=1).astype(np.float32)
    return both.astype(ml_dtypes.bfloat16)


def regroup_table(segs):
    per = LANES // GROUP
    table = np.zeros((segs, per, GROUP, per, segs, GROUP), np.float32)
    for s in range(segs):
        for q in range(per):
            for f in range(GROUP):
                table[s, q, f, q, s, f] = 1.0
    size = segs * LANES
    return table.reshape(size, size).astype(ml_dtypes.bfloat16)


def row_table(channels, segs):
    table = np.zeros((segs, channels, channels, segs), np.float32)
    for s in range(segs):
        for c in range(channels):
            table[s, c, c, s] = 1.0
    size = segs * channels
    return table.reshape(size, size).astype(ml_dtypes.bfloat16)


def mm(a, b):
    return jnp.dot(a, b, preferred_element_type=jnp.float32)


def mm_t(a, b):
    return lax.dot_general(a, b, (((1,), (1,)), ((), ())), preferred_element_type=jnp.float32)


def kernel(
    blks, grps, dims, normalise,
    rec_ref, flag_ref, hi_ref, lo_ref, perm_ref, row_ref, lag_ref,
    out_ref, count_ref,
    buf, diag, cross, inv, recv_sem, hop_sem, peer_sem, sib_sem,
):
    channels, segs, bins, half = dims
    width = half * 2 * segs
    chunks = half // GROUP
    pair = channels // 2
    b = lax.axis_index("blk")
    g = lax.axis_index("grp")
    sib = g + 1 - 2 * lax.rem(g, 2)
    peers = [lax.rem(g + 2 * d, grps) for d in range(1, grps // 2)]

    barrier = pltpu.get_barrier_semaphore()
    for k in range(1, STEPS):
        pl.semaphore_signal(barrier, inc=1, device_id={"blk": lax.rem(b + blks - k, blks)}, device_id_type=MESH)
    for other in peers + [sib]:
        pl.semaphore_signal(barrier, inc=1, device_id={"grp": other}, device_id_type=MESH)

    rec = mm(row_ref[...], rec_ref[...]).astype(jnp.bfloat16)
    spec = mm(rec, hi_ref[...]) + mm(rec, lo_ref[...])
    real = spec[:, :bins]
    imag = spec[:, bins:]
    power = real * real + imag * imag
    level = jnp.sum(power, axis=1, keepdims=True) / bins
    scale = 1.0 / jnp.sqrt(power[:, :half] + level + 1e-06)
    flags = flag_ref[...]
    pieces = [(real[:, :half] * scale).astype(jnp.bfloat16), (imag[:, :half] * scale).astype(jnp.bfloat16)]
    rows = []
    for t in range(half // LANES):
        for piece in pieces:
            rows.append(jnp.concatenate([
                piece[s * channels:(s + 1) * channels, t * LANES:(t + 1) * LANES]
                * flags[:, s:s + 1].astype(jnp.bfloat16)
                for s in range(segs)
            ], axis=1))
    regrouped = mm(jnp.concatenate(rows, axis=0), perm_ref[...]).astype(jnp.bfloat16)
    per = LANES // GROUP
    for t in range(half // LANES):
        for i in range(2):
            part = regrouped[(t * 2 + i) * channels:(t * 2 + i + 1) * channels]
            for q in range(per):
                at = ((t * per + q) * 2 + i) * LANES
                buf[0, g, :, at:at + LANES] = part[:, q * LANES:(q + 1) * LANES]
    buf[0, g, :, width:width + LANES] = flags.astype(jnp.bfloat16)

    pl.semaphore_wait(barrier, STEPS - 1 + len(peers) + 1)

    sent = []

    def send(source, k, slot, sem, where):
        copy = pltpu.make_async_remote_copy(
            src_ref=source, dst_ref=buf.at[k, slot], send_sem=sem,
            recv_sem=recv_sem.at[k, slot], device_id=where, device_id_type=MESH,
        )
        copy.start()
        sent.append(copy)

    def arrived(k, slot):
        pltpu.make_async_copy(buf.at[k, slot], buf.at[k, slot], recv_sem.at[k, slot]).wait()

    def spread(k):
        for d, other in enumerate(peers):
            send(buf.at[k, g], k, g, peer_sem.at[k, d], {"grp": other})
        send(buf.at[k, g], k, g, sib_sem.at[k, 0], {"grp": sib})

    def forward(k):
        for d in range(len(peers)):
            slot = lax.rem(g + grps - 2 * (d + 1), grps)
            arrived(k, slot)
            send(buf.at[k, slot], k, slot, sib_sem.at[k, d + 1], {"grp": sib})

    def gather(k):
        for d in range(grps // 2):
            arrived(k, lax.rem(sib + 2 * d, grps))

    for k in range(1, STEPS):
        send(buf.at[0, g], k, g, hop_sem.at[k], {"blk": lax.rem(b + k, blks)})
    spread(0)

    size = 2 * segs * GROUP
    same = (lax.broadcasted_iota(jnp.int32, (channels * GROUP, size), 0) % GROUP
            == lax.broadcasted_iota(jnp.int32, (channels * GROUP, size), 1) % GROUP)

    def build(q, carry):
        at = pl.multiple_of(q * size, size)
        first = buf[0, g, :, pl.ds(at, size)].astype(jnp.float32)
        second = jnp.concatenate([first[:, LANES:], -first[:, :LANES]], axis=1)
        for i, value in enumerate((first, second)):
            wide = jnp.broadcast_to(value[:, None, :], (channels, GROUP, size)).reshape(channels * GROUP, size)
            diag[q, i * channels * GROUP:(i + 1) * channels * GROUP, :] = jnp.where(same, wide, 0.0).astype(jnp.bfloat16)
        return carry

    lax.fori_loop(0, chunks // 2, build, 0)
    arrived(1, g)
    spread(1)
    forward(0)
    lax.fori_loop(chunks // 2, chunks, build, 0)
    arrived(2, g)
    spread(2)
    gather(0)

    block = grps * channels
    for k in range(STEPS):
        tile = buf[k, :, :, width:width + LANES].reshape(block, LANES)
        count = mm_t(flags.astype(jnp.bfloat16), tile)
        count_ref[:, k * block:(k + 1) * block] = count
        factor = lax.rsqrt(bins * jnp.maximum(count, 1.0))
        inv[:, :block] = factor[:pair]
        inv[:, block:] = factor[pair:]

        def multiply(q, carry, k=k):
            at = pl.multiple_of(q * size, size)
            other = buf[k, :, :, pl.ds(at, size)].reshape(block, size)
            product = mm_t(diag[q], other).astype(jnp.bfloat16).reshape(2, 2, pair, GROUP, block)
            low = pl.multiple_of(q * GROUP, GROUP)
            for i in range(2):
                for p in range(2):
                    cross[:, i, pl.ds(low, GROUP), p * block:(p + 1) * block] = product[i, p]
            return carry

        lax.fori_loop(0, chunks, multiply, 0)
        if k + 1 < STEPS:
            forward(k + 1)

        def lag(c, carry, k=k):
            total = mm(lag_ref[...], cross[c].reshape(2 * half, 2 * block)).astype(jnp.bfloat16)
            if normalise:
                total = (total.astype(jnp.float32) * inv[pl.ds(c, 1), :]).astype(jnp.bfloat16)
            out_ref[c, :, k * block:(k + 1) * block] = total[:, :block]
            out_ref[c + pair, :, k * block:(k + 1) * block] = total[:, block:]
            return carry

        lax.fori_loop(0, pair, lag, 0)
        if k + 1 < STEPS:
            gather(k + 1)

    for copy in sent:
        copy.wait_send()


def on_device(records, flags):
    channels, segs, length = records.shape
    bins = length // 2
    splits = lax.axis_size("sub")
    blks = lax.axis_size("blk")
    grps = lax.axis_size("grp")
    half = bins // splits
    block = grps * channels
    cos, sin = dft_tables(length)
    lags = lag_tables(length)
    both = np.stack([cos, sin], axis=1)
    high = both.astype(ml_dtypes.bfloat16)
    low = (both - high.astype(np.float32)).astype(ml_dtypes.bfloat16)
    high, low, lags = jnp.asarray(high), jnp.asarray(low), jnp.asarray(lags)
    if splits > 1:
        first = lax.axis_index("sub") * half
        high = jnp.roll(high, -first, axis=2)
        low = jnp.roll(low, -first, axis=2)
        lags = lax.dynamic_slice_in_dim(lags, first, half, 2)
    width = half * 2 * segs + LANES
    wide_flags = jnp.pad(flags.astype(jnp.float32), ((0, 0), (0, LANES - segs)))
    vmem = pl.BlockSpec(memory_space=pltpu.VMEM)
    out, count = pl.pallas_call(
        functools.partial(kernel, blks, grps, (channels, segs, bins, half), splits == 1),
        out_shape=(
            jax.ShapeDtypeStruct((channels, LAGS, STEPS * block), jnp.bfloat16),
            jax.ShapeDtypeStruct((channels, STEPS * block), jnp.float32),
        ),
        in_specs=[vmem] * 7,
        out_specs=(vmem, vmem),
        scratch_shapes=[
            pltpu.VMEM((STEPS, grps, channels, width), jnp.bfloat16),
            pltpu.VMEM((half // GROUP, 2 * channels * GROUP, 2 * segs * GROUP), jnp.bfloat16),
            pltpu.VMEM((channels // 2, 2, half, 2 * block), jnp.bfloat16),
            pltpu.VMEM((channels // 2, 2 * block), jnp.float32),
            pltpu.SemaphoreType.DMA((STEPS, grps)),
            pltpu.SemaphoreType.DMA((STEPS,)),
            pltpu.SemaphoreType.DMA((STEPS, max(grps // 2 - 1, 1))),
            pltpu.SemaphoreType.DMA((STEPS, grps // 2)),
        ],
        compiler_params=pltpu.CompilerParams(
            collective_id=0, has_side_effects=True, vmem_limit_bytes=48 * 1024 * 1024
        ),
    )(
        records.reshape(channels * segs, length),
        wide_flags,
        high.reshape(length, 2 * bins),
        low.reshape(length, 2 * bins),
        jnp.asarray(regroup_table(segs)),
        jnp.asarray(row_table(channels, segs)),
        lags.reshape(LAGS, 2 * half),
    )
    out = out.transpose(1, 0, 2)
    if splits > 1:
        out = lax.psum_scatter(out, "sub", scatter_dimension=0, tiled=True).astype(jnp.float32)
        out = (out / jnp.sqrt(bins * jnp.maximum(count, 1.0))[None]).astype(jnp.bfloat16)
    return out.reshape(-1, channels, STEPS, block)


def solution(mesh):
    return jax.shard_map(
        on_device,
        mesh=mesh,
        in_specs=(P(("dom", "blk", "grp"), None, None), P(("dom", "blk", "grp"), None)),
        out_specs=P("sub", ("dom", "blk", "grp"), None, None),
        check_vma=False,
    )
```

time: 176 us -> 71.9 us (0.41)
  waiting for transfers between devices: 95.4 us -> 0 us
  Pallas kernels: 0 us -> 58.3 us
  matrix products: 17.6 us -> 0 us
  between operations: 13.7 us -> 0.02 us
  other arithmetic: 13.9 us -> 0.69 us
  local copies, waits for them, and re-layouts: 23.2 us -> 12.5 us
  blocking collectives: 8.84 us -> 0 us
  starting transfers between devices: 3.2 us -> 0 us
    ppermute x4 -> x0, waiting for transfers between devices: 64.6 us -> none  [shifted(): return lax.ppermute(value, axis, pairs)]
    pallas_call x0 -> x1, Pallas kernels: none -> 58.3 us  [on_device(): pl.pallas_call(functools.partial(kernel, blks, grps, (channels, segs, bin...]
    all_gather x1 -> x0, waiting for transfers between devices: 30.7 us -> none  [on_device(): lax.all_gather(white, 'grp', axis=0, tiled=True)]
    dot_general x10 -> x0, matrix products: 17.6 us -> none  [the longest x3 10.4 us: on_device(): jnp.einsum('cisf,jsf->cijf', stacked, other.reshape(width, 2 * segs, half...]
    another operation x2 -> x0, local copies, waits for them, and re-layouts: 10.2 us -> none  [the longest x1 6.47 us: on_device(): jnp.stack([white.reshape(channels, 2 * segs, half), jnp.concatenate([whit...]
    reshape x3 -> x1, local copies, waits for them, and re-layouts: 12.7 us -> 3.28 us  [on_device(): return out.reshape(-1, channels, STEPS, block)]
    all_gather x1 -> x0, blocking collectives: 8.84 us -> none  [on_device(): lax.all_gather(own_flags, 'grp', axis=0, tiled=True)]
    neg x1 -> x0, other arithmetic: 8.24 us -> none  [on_device(): transform = jnp.concatenate([jnp.cos(angle), -jnp.sin(angle)], axis=1)]
  transfers between devices with their start and end apart: 5 -> 0, of which waited for: 4 -> 0; matrix products, arithmetic and copies ran while one was open for 18% -> 0% of each run, Pallas kernels for 0% -> 0%
where the time goes in v1:
time: 71.9 us; the launch traced here: 71.5 us
  Pallas kernels  58.3 us (81%)
  local copies, waits for them, and re-layouts  12.5 us (17%)
    pallas_call x1, Pallas kernels, on_device(): pl.pallas_call(functools.partial(kernel, blks, grps, (channels, segs, bin...  58.3 us
    unnamed x10, local copies, waits for them, and re-layouts  5.93 us
    reshape x1, local copies, waits for them, and re-layouts, on_device(): return out.reshape(-1, channels, STEPS, block)  3.28 us
    transpose x1, local copies, waits for them, and re-layouts, on_device(): out = out.transpose(1, 0, 2)  3.17 us

profile of v1, /device:TPU:0, one launch (start us, length us, event | category | flops | bytes accessed | tf_op | source)
XLA Modules:
  0.0 71.5 jit_solution(14866160069035587630)
XLA Ops:
  0.0 0.7 convert_element_type.5
  0.7 0.1 copy.13
  0.8 0.0 copy-start
  0.8 1.6 %copy-done = bf16[1024,1024]{1,0:T(8,128)(2,1)S(1)} copy-done((bf16[1024,1024]{1,0:T(8,128)(2,1)S(1)}, bf16[1024,1024]{1,0:T(8,128)(2,1)}, u32[]{:S(2)}) %copy-start) | copy-done | bytes 2097176
  2.4 0.0 copy-start.1
  2.4 1.6 %copy-done.1 = bf16[1024,1024]{1,0:T(8,128)(2,1)S(1)} copy-done((bf16[1024,1024]{1,0:T(8,128)(2,1)S(1)}, bf16[1024,1024]{1,0:T(8,128)(2,1)}, u32[]{:S(2)}) %copy-start.1) | copy-done | bytes 2097176
  4.0 0.0 copy-start.2
  4.0 1.0 %copy-done.2 = bf16[256,1024]{1,0:T(8,128)(2,1)S(1)} copy-done((bf16[256,1024]{1,0:T(8,128)(2,1)S(1)}, bf16[256,1024]{1,0:T(8,128)(2,1)}, u32[]{:S(2)}) %copy-start.2) | copy-done | bytes 524312
  5.0 0.0 copy-start.3
  5.0 0.9 %copy-done.3 = bf16[16,8,1024]{2,1,0:T(8,128)(2,1)S(1)} copy-done((bf16[16,8,1024]{2,1,0:T(8,128)(2,1)S(1)}, bf16[16,8,1024]{2,1,0:T(8,128)(2,1)}, u32[]{:S(2)}) %copy-start.3) | copy-done | bytes 262168
  5.9 0.0 copy-start.4
  6.0 0.8 %copy-done.4 = bf16[128,128]{1,0:T(8,128)(2,1)S(1)} copy-done((bf16[128,128]{1,0:T(8,128)(2,1)S(1)}, bf16[128,128]{1,0:T(8,128)(2,1)}, u32[]{:S(2)}) %copy-start.4) | copy-done | bytes 32792
  6.7 58.3 %shard_map.73 = (bf16[16,256,384]{2,1,0:T(8,128)(2,1)}, f32[16,384]{1,0:T(8,128)}) custom-call(bf16[128,1024]{1,0:T(8,128)(2,1)S(1)} %bitcast.3, f32[16,128]{1,0:T(8,128)S(1)} %pad.4.flag_ref, bf16[1024,1024]{1,0:T(8,128)(2,1)S(1)} %copy-done.1, bf16[1024,1024]{1,0:T(8,128)(2,1)S(1)} %copy-done, bf16[1024,1024]{1,0:T(8,128)(2,1)} %constant.16.clone.perm_ref, ...), custom_call_target="tpu_custom_call" | custom-call | tf_op jit(solution)/shard_map/pallas_call | solution.py:227
  65.0 3.2 %copy.14 = bf16[256,16,384]{0,2,1:T(8,128)(2,1)S(1)} copy(bf16[256,16,384]{2,0,1:T(8,128)(2,1)} %bitcast.5) | data formatting | bytes 6291456 | tf_op jit(solution)/shard_map/transpose | solution.py:257
  68.2 3.3 %copy.15 = bf16[256,16,3,128]{3,1,2,0:T(8,128)(2,1)} copy(bf16[256,16,3,128]{0,3,2,1:T(8,128)(2,1)S(1)} %bitcast.4) | data formatting | bytes 6291456 | tf_op jit(solution)/shard_map/reshape | solution.py:261
  (1 shorter events, 0.0 us)
Async XLA Ops:
  0.8 1.6 %copy-start = (bf16[1024,1024]{1,0:T(8,128)(2,1)S(1)}, bf16[1024,1024]{1,0:T(8,128)(2,1)}, u32[]{:S(2)}) copy-start(bf16[1024,1024]{1,0:T(8,128)(2,1)} %constant.23.lo_ref) | copy-start | bytes 6291460
  2.4 1.6 %copy-start.1 = (bf16[1024,1024]{1,0:T(8,128)(2,1)S(1)}, bf16[1024,1024]{1,0:T(8,128)(2,1)}, u32[]{:S(2)}) copy-start(bf16[1024,1024]{1,0:T(8,128)(2,1)} %constant.22.hi_ref) | copy-start | bytes 6291460
  4.0 1.0 %copy-start.2 = (bf16[256,1024]{1,0:T(8,128)(2,1)S(1)}, bf16[256,1024]{1,0:T(8,128)(2,1)}, u32[]{:S(2)}) copy-start(bf16[256,1024]{1,0:T(8,128)(2,1)} %constant.24.lag_ref) | copy-start | bytes 1572868
  5.0 0.9 %copy-start.3 = (bf16[16,8,1024]{2,1,0:T(8,128)(2,1)S(1)}, bf16[16,8,1024]{2,1,0:T(8,128)(2,1)}, u32[]{:S(2)}) copy-start(bf16[16,8,1024]{2,1,0:T(8,128)(2,1)} %param.7) | copy-start | bytes 786436
  5.9 0.8 %copy-start.4 = (bf16[128,128]{1,0:T(8,128)(2,1)S(1)}, bf16[128,128]{1,0:T(8,128)(2,1)}, u32[]{:S(2)}) copy-start(bf16[128,128]{1,0:T(8,128)(2,1)} %constant.17.clone.row_ref) | copy-start | bytes 98308

commit v2 on v1

--- a/solution.py
+++ b/solution.py
@@ -61,18 +61,29 @@
 
 def kernel(
     blks, grps, dims, normalise,
-    rec_ref, flag_ref, hi_ref, lo_ref, perm_ref, row_ref, lag_ref,
+    rec_ref, flag_ref, row_ref, hi_hbm, lo_hbm, perm_hbm, lag_hbm,
     out_ref, count_ref,
-    buf, diag, cross, inv, recv_sem, hop_sem, peer_sem, sib_sem,
+    hi_ref, lo_ref, perm_ref, lag_ref, load_sem, buf, diag, cross, inv, recv_sem, hop_sem, peer_sem,
 ):
     channels, segs, bins, half = dims
     width = half * 2 * segs
     chunks = half // GROUP
     pair = channels // 2
+    loads = [
+        pltpu.make_async_copy(source, target, load_sem.at[n])
+        for n, (source, target) in enumerate(
+            ((hi_hbm, hi_ref), (lo_hbm, lo_ref), (perm_hbm, perm_ref), (lag_hbm, lag_ref)))
+    ]
+    for load in loads:
+        load.start()
     b = lax.axis_index("blk")
     g = lax.axis_index("grp")
     sib = g + 1 - 2 * lax.rem(g, 2)
-    peers = [lax.rem(g + 2 * d, grps) for d in range(1, grps // 2)]
+    chip = g // 2
+    across = g + 2 - 4 * lax.rem(chip, 2)
+    along = g + 4 - 8 * (chip // 2)
+    corner = across + 4 - 8 * (chip // 2)
+    peers = [across, along]
 
     barrier = pltpu.get_barrier_semaphore()
     for k in range(1, STEPS):
@@ -81,7 +92,10 @@
         pl.semaphore_signal(barrier, inc=1, device_id={"grp": other}, device_id_type=MESH)
 
     rec = mm(row_ref[...], rec_ref[...]).astype(jnp.bfloat16)
-    spec = mm(rec, hi_ref[...]) + mm(rec, lo_ref[...])
+    loads[0].wait()
+    spec = mm(rec, hi_ref[...])
+    loads[1].wait()
+    spec = spec + mm(rec, lo_ref[...])
     real = spec[:, :bins]
     imag = spec[:, bins:]
     power = real * real + imag * imag
@@ -97,6 +111,7 @@
                 * flags[:, s:s + 1].astype(jnp.bfloat16)
                 for s in range(segs)
             ], axis=1))
+    loads[2].wait()
     regrouped = mm(jnp.concatenate(rows, axis=0), perm_ref[...]).astype(jnp.bfloat16)
     per = LANES // GROUP
     for t in range(half // LANES):
@@ -111,34 +126,63 @@
 
     sent = []
 
-    def send(source, k, slot, sem, where):
+    cut = width // 2
+    rest = width + LANES - cut
+
+    def send(source, target, sems, where):
         copy = pltpu.make_async_remote_copy(
-            src_ref=source, dst_ref=buf.at[k, slot], send_sem=sem,
-            recv_sem=recv_sem.at[k, slot], device_id=where, device_id_type=MESH,
+            src_ref=source, dst_ref=target, send_sem=sems[0], recv_sem=sems[1],
+            device_id=where, device_id_type=MESH,
         )
         copy.start()
         sent.append(copy)
 
-    def arrived(k, slot):
-        pltpu.make_async_copy(buf.at[k, slot], buf.at[k, slot], recv_sem.at[k, slot]).wait()
+    def arrived(ref, sem):
+        pltpu.make_async_copy(ref, ref, sem).wait()
+
+    def whole(k, slot):
+        return buf.at[k, slot]
+
+    def lower(k, slot):
+        return buf.at[k, slot, :, pl.ds(0, cut)]
+
+    def upper(k, slot):
+        return buf.at[k, slot, :, pl.ds(cut, rest)]
+
+    def to(kind, k):
+        return peer_sem.at[k, kind], recv_sem.at[k, kind]
+
+    def hand(k, kind, slot):
+        send(whole(k, slot), whole(k, slot), to(kind, k), {"grp": sib})
 
     def spread(k):
-        for d, other in enumerate(peers):
-            send(buf.at[k, g], k, g, peer_sem.at[k, d], {"grp": other})
-        send(buf.at[k, g], k, g, sib_sem.at[k, 0], {"grp": sib})
+        send(whole(k, g), whole(k, g), to(0, k), {"grp": across})
+        send(whole(k, g), whole(k, g), to(1, k), {"grp": along})
+        hand(k, 4, g)
+
+    def relay(k):
+        arrived(whole(k, across), recv_sem.at[k, 0])
+        send(lower(k, across), lower(k, across), to(2, k), {"grp": along})
+        hand(k, 5, across)
+        arrived(whole(k, along), recv_sem.at[k, 1])
+        send(upper(k, along), upper(k, along), to(3, k), {"grp": across})
+        hand(k, 6, along)
 
     def forward(k):
-        for d in range(len(peers)):
-            slot = lax.rem(g + grps - 2 * (d + 1), grps)
-            arrived(k, slot)
-            send(buf.at[k, slot], k, slot, sib_sem.at[k, d + 1], {"grp": sib})
+        arrived(lower(k, corner), recv_sem.at[k, 2])
+        arrived(upper(k, corner), recv_sem.at[k, 3])
+        hand(k, 7, corner)
 
     def gather(k):
-        for d in range(grps // 2):
-            arrived(k, lax.rem(sib + 2 * d, grps))
+        turn = sib - g
+        for kind, slot in ((4, g), (5, across), (6, along), (7, corner)):
+            arrived(whole(k, slot + turn), recv_sem.at[k, kind])
+
+    def hopped(k):
+        arrived(whole(k, g), hop_sem.at[1, k])
 
     for k in range(1, STEPS):
-        send(buf.at[0, g], k, g, hop_sem.at[k], {"blk": lax.rem(b + k, blks)})
+        send(whole(0, g), whole(k, g), (hop_sem.at[0, k], hop_sem.at[1, k]), {"blk": lax.rem(b + k, blks)})
     spread(0)
 
     size = 2 * segs * GROUP
@@ -155,14 +199,17 @@
         return carry
 
     lax.fori_loop(0, chunks // 2, build, 0)
-    arrived(1, g)
+    relay(0)
+    hopped(1)
     spread(1)
+    lax.fori_loop(chunks // 2, chunks, build, 0)
     forward(0)
-    lax.fori_loop(chunks // 2, chunks, build, 0)
-    arrived(2, g)
+    hopped(2)
     spread(2)
+    relay(1)
     gather(0)
 
+    loads[3].wait()
     block = grps * channels
     for k in range(STEPS):
         tile = buf[k, :, :, width:width + LANES].reshape(block, LANES)
@@ -184,14 +231,16 @@
 
         lax.fori_loop(0, chunks, multiply, 0)
         if k + 1 < STEPS:
+            if k > 0:
+                relay(k + 1)
             forward(k + 1)
 
         def lag(c, carry, k=k):
             total = mm(lag_ref[...], cross[c].reshape(2 * half, 2 * block)).astype(jnp.bfloat16)
             if normalise:
                 total = (total.astype(jnp.float32) * inv[pl.ds(c, 1), :]).astype(jnp.bfloat16)
-            out_ref[c, :, k * block:(k + 1) * block] = total[:, :block]
-            out_ref[c + pair, :, k * block:(k + 1) * block] = total[:, block:]
+            out_ref[k, c] = total[:, :block]
+            out_ref[k, c + pair] = total[:, block:]
             return carry
 
         lax.fori_loop(0, pair, lag, 0)
@@ -227,38 +276,42 @@
     out, count = pl.pallas_call(
         functools.partial(kernel, blks, grps, (channels, segs, bins, half), splits == 1),
         out_shape=(
-            jax.ShapeDtypeStruct((channels, LAGS, STEPS * block), jnp.bfloat16),
+            jax.ShapeDtypeStruct((STEPS, channels, LAGS, block), jnp.bfloat16),
             jax.ShapeDtypeStruct((channels, STEPS * block), jnp.float32),
         ),
-        in_specs=[vmem] * 7,
+        in_specs=[vmem] * 3 + [pl.BlockSpec(memory_space=pltpu.HBM)] * 4,
         out_specs=(vmem, vmem),
         scratch_shapes=[
+            pltpu.VMEM((length, 2 * bins), jnp.bfloat16),
+            pltpu.VMEM((length, 2 * bins), jnp.bfloat16),
+            pltpu.VMEM((segs * LANES, segs * LANES), jnp.bfloat16),
+            pltpu.VMEM((LAGS, 2 * half), jnp.bfloat16),
+            pltpu.SemaphoreType.DMA((4,)),
             pltpu.VMEM((STEPS, grps, channels, width), jnp.bfloat16),
             pltpu.VMEM((half // GROUP, 2 * channels * GROUP, 2 * segs * GROUP), jnp.bfloat16),
             pltpu.VMEM((channels // 2, 2, half, 2 * block), jnp.bfloat16),
             pltpu.VMEM((channels // 2, 2 * block), jnp.float32),
-            pltpu.SemaphoreType.DMA((STEPS, grps)),
-            pltpu.SemaphoreType.DMA((STEPS,)),
-            pltpu.SemaphoreType.DMA((STEPS, max(grps // 2 - 1, 1))),
-            pltpu.SemaphoreType.DMA((STEPS, grps // 2)),
+            pltpu.SemaphoreType.DMA((STEPS, 8)),
+            pltpu.SemaphoreType.DMA((2, STEPS)),
+            pltpu.SemaphoreType.DMA((STEPS, 8)),
         ],
         compiler_params=pltpu.CompilerParams(
-            collective_id=0, has_side_effects=True, vmem_limit_bytes=48 * 1024 * 1024
+            collective_id=0, has_side_effects=True, vmem_limit_bytes=62 * 1024 * 1024
         ),
     )(
         records.reshape(channels * segs, length),
         wide_flags,
+        jnp.asarray(row_table(channels, segs)),
         high.reshape(length, 2 * bins),
         low.reshape(length, 2 * bins),
         jnp.asarray(regroup_table(segs)),
-        jnp.asarray(row_table(channels, segs)),
         lags.reshape(LAGS, 2 * half),
     )
-    out = out.transpose(1, 0, 2)
+    out = out.transpose(2, 1, 0, 3)
     if splits > 1:
         out = lax.psum_scatter(out, "sub", scatter_dimension=0, tiled=True).astype(jnp.float32)
-        out = (out / jnp.sqrt(bins * jnp.maximum(count, 1.0))[None]).astype(jnp.bfloat16)
-    return out.reshape(-1, channels, STEPS, block)
+        out = (out / jnp.sqrt(bins * jnp.maximum(count, 1.0)).reshape(1, channels, STEPS, block)).astype(jnp.bfloat16)
+    return out
 
 
 def solution(mesh):

time: 71.9 us -> 73.2 us (1.018)
  Pallas kernels: 58.3 us -> 66 us
  local copies, waits for them, and re-layouts: 12.5 us -> 6.26 us
    pallas_call x1, Pallas kernels: 58.3 us -> 66 us  [on_device(): pl.pallas_call(functools.partial(kernel, blks, grps, (channels, segs, bin...]
    unnamed x10 -> x0, local copies, waits for them, and re-layouts: 5.93 us -> none
    reshape x1 -> x0, local copies, waits for them, and re-layouts: 3.28 us -> none  [on_device(): return out.reshape(-1, channels, STEPS, block)]
    transpose x1, local copies, waits for them, and re-layouts: 3.17 us -> 5.58 us  [on_device(): out = out.transpose(2, 1, 0, 3)]
where the time goes in v2:
time: 73.2 us; the launch traced here: 73 us
  Pallas kernels  66 us (90%)
  local copies, waits for them, and re-layouts  6.26 us (9%)
    pallas_call x1, Pallas kernels, on_device(): pl.pallas_call(functools.partial(kernel, blks, grps, (channels, segs, bin...  66 us
    transpose x1, local copies, waits for them, and re-layouts, on_device(): out = out.transpose(2, 1, 0, 3)  5.58 us

profile of v2, /device:TPU:0, one launch (start us, length us, event | category | flops | bytes accessed | tf_op | source)
XLA Modules:
  0.0 73.0 jit_solution(7906628263351324128)
XLA Ops:
  0.0 0.7 convert_element_type.5
  0.7 0.1 copy.10
  0.8 0.6 pad.4.flag_ref
  1.4 66.0 %shard_map.73 = (bf16[3,16,256,128]{3,2,1,0:T(8,128)(2,1)}, f32[16,384]{1,0:T(8,128)}) custom-call(bf16[128,1024]{1,0:T(8,128)(2,1)} %bitcast.3, f32[16,128]{1,0:T(8,128)} %pad.4.flag_ref, bf16[128,128]{1,0:T(8,128)(2,1)} %constant.16.clone.row_ref, bf16[1024,1024]{1,0:T(8,128)(2,1)} %constant.22.hi_hbm, bf16[1024,1024]{1,0:T(8,128)(2,1)} %constant.23.lo_hbm, ...), custom_call_target="tpu_custom_call" | custom-call | tf_op jit(solution)/shard_map/pallas_call | solution.py:276
  67.4 5.6 %copy.11 = bf16[256,16,3,128]{3,1,2,0:T(8,128)(2,1)} copy(bf16[256,16,3,128]{3,0,1,2:T(8,128)(2,1)} %bitcast.2) | data formatting | bytes 6291456 | tf_op jit(solution)/shard_map/transpose | solution.py:310

commit v3 on v2

--- a/solution.py
+++ b/solution.py
@@ -63,7 +63,7 @@
     blks, grps, dims, normalise,
     rec_ref, flag_ref, row_ref, hi_hbm, lo_hbm, perm_hbm, lag_hbm,
     out_ref, count_ref,
-    hi_ref, lo_ref, perm_ref, lag_ref, load_sem, buf, diag, cross, inv, recv_sem, hop_sem, peer_sem,
+    hi_ref, lo_ref, perm_ref, lag_ref, load_sem, buf, diag, cross, inv, recv_sem, hop_sem, peer_sem, sib_sem,
 ):
     channels, segs, bins, half = dims
     width = half * 2 * segs
@@ -79,11 +79,7 @@
     b = lax.axis_index("blk")
     g = lax.axis_index("grp")
     sib = g + 1 - 2 * lax.rem(g, 2)
-    chip = g // 2
-    across = g + 2 - 4 * lax.rem(chip, 2)
-    along = g + 4 - 8 * (chip // 2)
-    corner = across + 4 - 8 * (chip // 2)
-    peers = [across, along]
+    peers = [lax.rem(g + 2 * d, grps) for d in range(1, grps // 2)]
 
     barrier = pltpu.get_barrier_semaphore()
     for k in range(1, STEPS):
@@ -127,63 +123,55 @@
     sent = []
 
     cut = width // 2
-    rest = width + LANES - cut
-
-    def send(source, target, sems, where):
+    spans = [(0, cut), (cut, width + LANES - cut)]
+    steps = [(k, h) for k in range(STEPS) for h in range(2)]
+
+    def piece(k, h, slot):
+        return buf.at[k, slot, :, pl.ds(*spans[h])]
+
+    def send(source, target, send_sem, landed, where):
         copy = pltpu.make_async_remote_copy(
-            src_ref=source, dst_ref=target, send_sem=sems[0], recv_sem=sems[1],
+            src_ref=source, dst_ref=target, send_sem=send_sem, recv_sem=landed,
             device_id=where, device_id_type=MESH,
         )
         copy.start()
         sent.append(copy)
 
-    def arrived(ref, sem):
-        pltpu.make_async_copy(ref, ref, sem).wait()
-
-    def whole(k, slot):
-        return buf.at[k, slot]
-
-    def lower(k, slot):
-        return buf.at[k, slot, :, pl.ds(0, cut)]
-
-    def upper(k, slot):
-        return buf.at[k, slot, :, pl.ds(cut, rest)]
-
-    def to(kind, k):
-        return peer_sem.at[k, kind], recv_sem.at[k, kind]
-
-    def hand(k, kind, slot):
-        send(whole(k, slot), whole(k, slot), to(kind, k), {"grp": sib})
-
-    def spread(k):
-        send(whole(k, g), whole(k, g), to(0, k), {"grp": across})
-        send(whole(k, g), whole(k, g), to(1, k), {"grp": along})
-        hand(k, 4, g)
-
-    def relay(k):
-        arrived(whole(k, across), recv_sem.at[k, 0])
-        send(lower(k, across), lower(k, across), to(2, k), {"grp": along})
-        hand(k, 5, across)
-        arrived(whole(k, along), recv_sem.at[k, 1])
-        send(upper(k, along), upper(k, along), to(3, k), {"grp": across})
-        hand(k, 6, along)
-
-    def forward(k):
-        arrived(lower(k, corner), recv_sem.at[k, 2])
-        arrived(upper(k, corner), recv_sem.at[k, 3])
-        hand(k, 7, corner)
-
-    def gather(k):
-        turn = sib - g
-        for kind, slot in ((4, g), (5, across), (6, along), (7, corner)):
-            arrived(whole(k, slot + turn), recv_sem.at[k, kind])
+    def arrived(k, h, slot):
+        ref = piece(k, h, slot)
+        pltpu.make_async_copy(ref, ref, recv_sem.at[k, h, slot]).wait()
+
+    def hand(k, h, slot, n):
+        ref = piece(k, h, slot)
+        send(ref, ref, sib_sem.at[k, h, n], recv_sem.at[k, h, slot], {"grp": sib})
+
+    def spread(k, h):
+        ref = piece(k, h, g)
+        for d, other in enumerate(peers):
+            send(ref, ref, peer_sem.at[k, h, d], recv_sem.at[k, h, g], {"grp": other})
+        hand(k, h, g, 0)
 
     def hopped(k):
-        arrived(whole(k, g), hop_sem.at[1, k])
-
+        for h in range(2):
+            arrived(k, h, g)
+            spread(k, h)
+
+    def forward(k, h):
+        for d in range(len(peers)):
+            slot = lax.rem(g + grps - 2 * (d + 1), grps)
+            arrived(k, h, slot)
+            hand(k, h, slot, d + 1)
+
+    def gather(k, h):
+        for d in range(grps // 2):
+            arrived(k, h, lax.rem(sib + 2 * d, grps))
+
+    spread(0, 0)
     for k in range(1, STEPS):
-        send(whole(0, g), whole(k, g), (hop_sem.at[0, k], hop_sem.at[1, k]), {"blk": lax.rem(b + k, blks)})
-    spread(0)
+        for h in range(2):
+            send(piece(0, h, g), piece(k, h, g), hop_sem.at[k, h], recv_sem.at[k, h, g],
+                 {"blk": lax.rem(b + k, blks)})
+    spread(0, 1)
 
     size = 2 * segs * GROUP
     same = (lax.broadcasted_iota(jnp.int32, (channels * GROUP, size), 0) % GROUP
@@ -199,27 +187,18 @@
         return carry
 
     lax.fori_loop(0, chunks // 2, build, 0)
-    relay(0)
     hopped(1)
-    spread(1)
+    forward(0, 0)
     lax.fori_loop(chunks // 2, chunks, build, 0)
-    forward(0)
     hopped(2)
-    spread(2)
-    relay(1)
-    gather(0)
-
+    forward(0, 1)
     loads[3].wait()
     block = grps * channels
-    for k in range(STEPS):
-        tile = buf[k, :, :, width:width + LANES].reshape(block, LANES)
-        count = mm_t(flags.astype(jnp.bfloat16), tile)
-        count_ref[:, k * block:(k + 1) * block] = count
-        factor = lax.rsqrt(bins * jnp.maximum(count, 1.0))
-        inv[:, :block] = factor[:pair]
-        inv[:, block:] = factor[pair:]
-
-        def multiply(q, carry, k=k):
+    unroll = 4
+
+    def multiply(group, carry, k):
+        for u in range(unroll):
+            q = group * unroll + u
             at = pl.multiple_of(q * size, size)
             other = buf[k, :, :, pl.ds(at, size)].reshape(block, size)
             product = mm_t(diag[q], other).astype(jnp.bfloat16).reshape(2, 2, pair, GROUP, block)
@@ -227,25 +206,30 @@
             for i in range(2):
                 for p in range(2):
                     cross[:, i, pl.ds(low, GROUP), p * block:(p + 1) * block] = product[i, p]
-            return carry
-
-        lax.fori_loop(0, chunks, multiply, 0)
-        if k + 1 < STEPS:
-            if k > 0:
-                relay(k + 1)
-            forward(k + 1)
-
-        def lag(c, carry, k=k):
-            total = mm(lag_ref[...], cross[c].reshape(2 * half, 2 * block)).astype(jnp.bfloat16)
-            if normalise:
-                total = (total.astype(jnp.float32) * inv[pl.ds(c, 1), :]).astype(jnp.bfloat16)
-            out_ref[k, c] = total[:, :block]
-            out_ref[k, c + pair] = total[:, block:]
-            return carry
-
-        lax.fori_loop(0, pair, lag, 0)
-        if k + 1 < STEPS:
-            gather(k + 1)
+        return carry
+
+    def lag(c, carry, k):
+        total = mm(lag_ref[...], cross[c].reshape(2 * half, 2 * block)).astype(jnp.bfloat16)
+        if normalise:
+            total = (total.astype(jnp.float32) * inv[pl.ds(c, 1), :]).astype(jnp.bfloat16)
+        out_ref[k, c] = total[:, :block]
+        out_ref[k, c + pair] = total[:, block:]
+        return carry
+
+    groups = chunks // 2 // unroll
+    for n, (k, h) in enumerate(steps):
+        gather(k, h)
+        lax.fori_loop(h * groups, (h + 1) * groups, functools.partial(multiply, k=k), 0)
+        if n + 2 < len(steps):
+            forward(*steps[n + 2])
+        if h == 1:
+            tile = buf[k, :, :, width:width + LANES].reshape(block, LANES)
+            count = mm_t(flags.astype(jnp.bfloat16), tile)
+            count_ref[:, k * block:(k + 1) * block] = count
+            factor = lax.rsqrt(bins * jnp.maximum(count, 1.0))
+            inv[:, :block] = factor[:pair]
+            inv[:, block:] = factor[pair:]
+            lax.fori_loop(0, pair, functools.partial(lag, k=k), 0)
 
     for copy in sent:
         copy.wait_send()
@@ -291,9 +275,10 @@
             pltpu.VMEM((half // GROUP, 2 * channels * GROUP, 2 * segs * GROUP), jnp.bfloat16),
             pltpu.VMEM((channels // 2, 2, half, 2 * block), jnp.bfloat16),
             pltpu.VMEM((channels // 2, 2 * block), jnp.float32),
-            pltpu.SemaphoreType.DMA((STEPS, 8)),
-            pltpu.SemaphoreType.DMA((2, STEPS)),
-            pltpu.SemaphoreType.DMA((STEPS, 8)),
+            pltpu.SemaphoreType.DMA((STEPS, 2, grps)),
+            pltpu.SemaphoreType.DMA((STEPS, 2)),
+            pltpu.SemaphoreType.DMA((STEPS, 2, max(grps // 2 - 1, 1))),
+            pltpu.SemaphoreType.DMA((STEPS, 2, grps // 2)),
         ],
         compiler_params=pltpu.CompilerParams(
             collective_id=0, has_side_effects=True, vmem_limit_bytes=62 * 1024 * 1024

time: 73.2 us -> 61.4 us (0.84)
  Pallas kernels: 66 us -> 54.3 us
    pallas_call x1, Pallas kernels: 66 us -> 54.3 us  [on_device(): pl.pallas_call(functools.partial(kernel, blks, grps, (channels, segs, bin...]
where the time goes in v3:
time: 61.4 us; the launch traced here: 61.3 us
  Pallas kernels  54.3 us (88%)
  local copies, waits for them, and re-layouts  6.26 us (10%)
  other arithmetic  0.69 us (1%)
    pallas_call x1, Pallas kernels, on_device(): pl.pallas_call(functools.partial(kernel, blks, grps, (channels, segs, bin...  54.3 us
    transpose x1, local copies, waits for them, and re-layouts, on_device(): out = out.transpose(2, 1, 0, 3)  5.58 us

profile of v3, /device:TPU:0, one launch (start us, length us, event | category | flops | bytes accessed | tf_op | source)
XLA Modules:
  0.0 61.3 jit_solution(6452542174870708757)
XLA Ops:
  0.0 0.7 %convert_element_type.5 = f32[16,8]{0,1:T(8,128)S(1)} convert(s32[16,8]{0,1:T(8,128)} %param.8) | non-fusion elementwise | flops 128 | bytes 1024 | tf_op jit(solution)/shard_map/convert_element_type | solution.py:258
  0.7 0.1 copy.10
  0.8 0.6 pad.4.flag_ref
  1.4 54.3 %shard_map.73 = (bf16[3,16,256,128]{3,2,1,0:T(8,128)(2,1)}, f32[16,384]{1,0:T(8,128)}) custom-call(bf16[128,1024]{1,0:T(8,128)(2,1)} %bitcast.3, f32[16,128]{1,0:T(8,128)} %pad.4.flag_ref, bf16[128,128]{1,0:T(8,128)(2,1)} %constant.16.clone.row_ref, bf16[1024,1024]{1,0:T(8,128)(2,1)} %constant.22.hi_hbm, bf16[1024,1024]{1,0:T(8,128)(2,1)} %constant.23.lo_hbm, ...), custom_call_target="tpu_custom_call" | custom-call | tf_op jit(solution)/shard_map/pallas_call | solution.py:260
  55.7 5.6 %copy.11 = bf16[256,16,3,128]{3,1,2,0:T(8,128)(2,1)} copy(bf16[256,16,3,128]{3,0,1,2:T(8,128)(2,1)} %bitcast.2) | data formatting | bytes 6291456 | tf_op jit(solution)/shard_map/transpose | solution.py:295

commit v4 on v3

--- a/solution.py
+++ b/solution.py
@@ -63,7 +63,7 @@
     blks, grps, dims, normalise,
     rec_ref, flag_ref, row_ref, hi_hbm, lo_hbm, perm_hbm, lag_hbm,
     out_ref, count_ref,
-    hi_ref, lo_ref, perm_ref, lag_ref, load_sem, buf, diag, cross, inv, recv_sem, hop_sem, peer_sem, sib_sem,
+    hi_ref, lo_ref, perm_ref, lag_ref, load_sem, buf, diag, cross, inv, stage, recv_sem, hop_sem, peer_sem, sib_sem,
 ):
     channels, segs, bins, half = dims
     width = half * 2 * segs
@@ -212,8 +212,15 @@
         total = mm(lag_ref[...], cross[c].reshape(2 * half, 2 * block)).astype(jnp.bfloat16)
         if normalise:
             total = (total.astype(jnp.float32) * inv[pl.ds(c, 1), :]).astype(jnp.bfloat16)
-        out_ref[k, c] = total[:, :block]
-        out_ref[k, c + pair] = total[:, block:]
+        total = total.astype(jnp.float32)
+        stage[pl.ds(c, LAGS, stride=channels), :] = total[:, :block]
+        stage[pl.ds(c + pair, LAGS, stride=channels), :] = total[:, block:]
+        return carry
+
+    def place(n, carry, k):
+        low = pl.multiple_of(n * 16, 16)
+        part = stage[pl.ds(pl.multiple_of(n * 16 * channels, 16), 16 * channels), :]
+        out_ref[pl.ds(low, 16), k] = part.astype(jnp.bfloat16).reshape(16, channels, block)
         return carry
 
     groups = chunks // 2 // unroll
@@ -230,6 +237,7 @@
             inv[:, :block] = factor[:pair]
             inv[:, block:] = factor[pair:]
             lax.fori_loop(0, pair, functools.partial(lag, k=k), 0)
+            lax.fori_loop(0, LAGS // 16, functools.partial(place, k=k), 0)
 
     for copy in sent:
         copy.wait_send()
@@ -260,7 +268,7 @@
     out, count = pl.pallas_call(
         functools.partial(kernel, blks, grps, (channels, segs, bins, half), splits == 1),
         out_shape=(
-            jax.ShapeDtypeStruct((STEPS, channels, LAGS, block), jnp.bfloat16),
+            jax.ShapeDtypeStruct((LAGS, STEPS, channels, block), jnp.bfloat16),
             jax.ShapeDtypeStruct((channels, STEPS * block), jnp.float32),
         ),
         in_specs=[vmem] * 3 + [pl.BlockSpec(memory_space=pltpu.HBM)] * 4,
@@ -275,6 +283,7 @@
             pltpu.VMEM((half // GROUP, 2 * channels * GROUP, 2 * segs * GROUP), jnp.bfloat16),
             pltpu.VMEM((channels // 2, 2, half, 2 * block), jnp.bfloat16),
             pltpu.VMEM((channels // 2, 2 * block), jnp.float32),
+            pltpu.VMEM(((LAGS + 1) * channels, block), jnp.float32),
             pltpu.SemaphoreType.DMA((STEPS, 2, grps)),
             pltpu.SemaphoreType.DMA((STEPS, 2)),
             pltpu.SemaphoreType.DMA((STEPS, 2, max(grps // 2 - 1, 1))),
@@ -292,7 +301,7 @@
         jnp.asarray(regroup_table(segs)),
         lags.reshape(LAGS, 2 * half),
     )
-    out = out.transpose(2, 1, 0, 3)
+    out = out.transpose(0, 2, 1, 3)
     if splits > 1:
         out = lax.psum_scatter(out, "sub", scatter_dimension=0, tiled=True).astype(jnp.float32)
         out = (out / jnp.sqrt(bins * jnp.maximum(count, 1.0)).reshape(1, channels, STEPS, block)).astype(jnp.bfloat16)

time: 61.4 us -> 60.9 us (level)
  local copies, waits for them, and re-layouts: 6.26 us -> 4.77 us
  Pallas kernels: 54.3 us -> 55.2 us
    transpose x1 -> x0, local copies, waits for them, and re-layouts: 5.58 us -> none  [on_device(): out = out.transpose(2, 1, 0, 3)]
    unnamed x0 -> x1, local copies, waits for them, and re-layouts: none -> 4.09 us
    pallas_call x1, Pallas kernels: 54.3 us -> 55.2 us  [on_device(): pl.pallas_call(functools.partial(kernel, blks, grps, (channels, segs, bin...]
where the time goes in v4:
time: 60.9 us; the launch traced here: 60.7 us
  Pallas kernels  55.2 us (91%)
  local copies, waits for them, and re-layouts  4.77 us (8%)
  other arithmetic  0.69 us (1%)
    pallas_call x1, Pallas kernels, on_device(): pl.pallas_call(functools.partial(kernel, blks, grps, (channels, segs, bin...  55.2 us
    unnamed x1, local copies, waits for them, and re-layouts  4.09 us

profile of v4, /device:TPU:0, one launch (start us, length us, event | category | flops | bytes accessed | tf_op | source)
XLA Modules:
  0.0 60.7 jit_solution(15764124971447898986)
XLA Ops:
  0.0 0.7 %convert_element_type.5 = f32[16,8]{0,1:T(8,128)S(1)} convert(s32[16,8]{0,1:T(8,128)} %param.8) | non-fusion elementwise | flops 128 | bytes 1024 | tf_op jit(solution)/shard_map/convert_element_type | solution.py:266
  0.7 0.1 copy.9
  0.8 0.6 pad.4.flag_ref
  1.4 55.2 %shard_map.73 = (bf16[256,3,16,128]{3,2,1,0:T(8,128)(2,1)}, f32[16,384]{1,0:T(8,128)}) custom-call(bf16[128,1024]{1,0:T(8,128)(2,1)} %bitcast.3, f32[16,128]{1,0:T(8,128)} %pad.4.flag_ref, bf16[128,128]{1,0:T(8,128)(2,1)} %constant.16.clone.row_ref, bf16[1024,1024]{1,0:T(8,128)(2,1)} %constant.22.hi_hbm, bf16[1024,1024]{1,0:T(8,128)(2,1)} %constant.23.lo_hbm, ...), custom_call_target="tpu_custom_call" | custom-call | tf_op jit(solution)/shard_map/pallas_call | solution.py:268
  56.6 4.1 %copy.11 = bf16[256,16,3,128]{3,1,2,0:T(8,128)(2,1)} copy(bf16[256,16,3,128]{3,1,2,0:T(8,128)(2,1)} %bitcast.2) | data formatting | bytes 6291456

commit v5 on v4

--- a/solution.py
+++ b/solution.py
@@ -227,8 +227,6 @@
     for n, (k, h) in enumerate(steps):
         gather(k, h)
         lax.fori_loop(h * groups, (h + 1) * groups, functools.partial(multiply, k=k), 0)
-        if n + 2 < len(steps):
-            forward(*steps[n + 2])
         if h == 1:
             tile = buf[k, :, :, width:width + LANES].reshape(block, LANES)
             count = mm_t(flags.astype(jnp.bfloat16), tile)
@@ -238,6 +236,8 @@
             inv[:, block:] = factor[pair:]
             lax.fori_loop(0, pair, functools.partial(lag, k=k), 0)
             lax.fori_loop(0, LAGS // 16, functools.partial(place, k=k), 0)
+        if 0 < n < len(steps) - 1:
+            forward(*steps[n + 1])
 
     for copy in sent:
         copy.wait_send()

time: 60.9 us -> 61.1 us (level)
  no operation moved by 1% of the time
where the time goes in v5:
time: 61.1 us; the launch traced here: 60.9 us
  Pallas kernels  55.4 us (91%)
  local copies, waits for them, and re-layouts  4.77 us (8%)
  other arithmetic  0.69 us (1%)
    pallas_call x1, Pallas kernels, on_device(): pl.pallas_call(functools.partial(kernel, blks, grps, (channels, segs, bin...  55.4 us
    unnamed x1, local copies, waits for them, and re-layouts  4.09 us

profile of v5, /device:TPU:0, one launch (start us, length us, event | category | flops | bytes accessed | tf_op | source)
XLA Modules:
  0.0 60.9 jit_solution(12635198919071411314)
XLA Ops:
  0.0 0.7 %convert_element_type.5 = f32[16,8]{0,1:T(8,128)S(1)} convert(s32[16,8]{0,1:T(8,128)} %param.8) | non-fusion elementwise | flops 128 | bytes 1024 | tf_op jit(solution)/shard_map/convert_element_type | solution.py:266
  0.7 0.1 copy.9
  0.8 0.6 pad.4.flag_ref
  1.4 55.4 %shard_map.73 = (bf16[256,3,16,128]{3,2,1,0:T(8,128)(2,1)}, f32[16,384]{1,0:T(8,128)}) custom-call(bf16[128,1024]{1,0:T(8,128)(2,1)} %bitcast.3, f32[16,128]{1,0:T(8,128)} %pad.4.flag_ref, bf16[128,128]{1,0:T(8,128)(2,1)} %constant.16.clone.row_ref, bf16[1024,1024]{1,0:T(8,128)(2,1)} %constant.22.hi_hbm, bf16[1024,1024]{1,0:T(8,128)(2,1)} %constant.23.lo_hbm, ...), custom_call_target="tpu_custom_call" | custom-call | tf_op jit(solution)/shard_map/pallas_call | solution.py:268
  56.8 4.1 %copy.11 = bf16[256,16,3,128]{3,1,2,0:T(8,128)(2,1)} copy(bf16[256,16,3,128]{3,1,2,0:T(8,128)(2,1)} %bitcast.2) | data formatting | bytes 6291456

commit v6 on v4

--- a/solution.py
+++ b/solution.py
@@ -63,7 +63,7 @@
     blks, grps, dims, normalise,
     rec_ref, flag_ref, row_ref, hi_hbm, lo_hbm, perm_hbm, lag_hbm,
     out_ref, count_ref,
-    hi_ref, lo_ref, perm_ref, lag_ref, load_sem, buf, diag, cross, inv, stage, recv_sem, hop_sem, peer_sem, sib_sem,
+    hi_ref, lo_ref, perm_ref, lag_ref, load_sem, buf, diag, cross, inv, wide, stage, recv_sem, hop_sem, peer_sem, sib_sem,
 ):
     channels, segs, bins, half = dims
     width = half * 2 * segs
@@ -97,7 +97,9 @@
     power = real * real + imag * imag
     level = jnp.sum(power, axis=1, keepdims=True) / bins
     scale = 1.0 / jnp.sqrt(power[:, :half] + level + 1e-06)
-    flags = flag_ref[...]
+    wide[...] = jnp.zeros_like(wide)
+    wide[:, :segs] = flag_ref[...].astype(jnp.float32)
+    flags = wide[...]
     pieces = [(real[:, :half] * scale).astype(jnp.bfloat16), (imag[:, :half] * scale).astype(jnp.bfloat16)]
     rows = []
     for t in range(half // LANES):
@@ -263,7 +265,6 @@
         low = jnp.roll(low, -first, axis=2)
         lags = lax.dynamic_slice_in_dim(lags, first, half, 2)
     width = half * 2 * segs + LANES
-    wide_flags = jnp.pad(flags.astype(jnp.float32), ((0, 0), (0, LANES - segs)))
     vmem = pl.BlockSpec(memory_space=pltpu.VMEM)
     out, count = pl.pallas_call(
         functools.partial(kernel, blks, grps, (channels, segs, bins, half), splits == 1),
@@ -283,6 +284,7 @@
             pltpu.VMEM((half // GROUP, 2 * channels * GROUP, 2 * segs * GROUP), jnp.bfloat16),
             pltpu.VMEM((channels // 2, 2, half, 2 * block), jnp.bfloat16),
             pltpu.VMEM((channels // 2, 2 * block), jnp.float32),
+            pltpu.VMEM((channels, LANES), jnp.float32),
             pltpu.VMEM(((LAGS + 1) * channels, block), jnp.float32),
             pltpu.SemaphoreType.DMA((STEPS, 2, grps)),
             pltpu.SemaphoreType.DMA((STEPS, 2)),
@@ -294,7 +296,7 @@
         ),
     )(
         records.reshape(channels * segs, length),
-        wide_flags,
+        flags,
         jnp.asarray(row_table(channels, segs)),
         high.reshape(length, 2 * bins),
         low.reshape(length, 2 * bins),

time: 60.9 us -> 60.9 us (level)
  other arithmetic: 0.69 us -> 0 us
  local copies, waits for them, and re-layouts: 4.77 us -> 5.45 us
    unnamed x1 -> x2, local copies, waits for them, and re-layouts: 4.09 us -> 5.45 us
    convert_element_type x1 -> x0, other arithmetic: 0.69 us -> none  [on_device(): wide_flags = jnp.pad(flags.astype(jnp.float32), ((0, 0), (0, LANES - segs)))]
where the time goes in v6:
time: 60.9 us; the launch traced here: 60.7 us
  Pallas kernels  55.2 us (91%)
  local copies, waits for them, and re-layouts  5.45 us (9%)
    pallas_call x1, Pallas kernels, on_device(): pl.pallas_call(functools.partial(kernel, blks, grps, (channels, segs, bin...  55.2 us
    unnamed x2, local copies, waits for them, and re-layouts  5.45 us

profile of v6, /device:TPU:0, one launch (start us, length us, event | category | flops | bytes accessed | tf_op | source)
XLA Modules:
  0.0 60.7 jit_solution(8601985562424321351)
XLA Ops:
  0.0 1.4 %copy.8.flag_ref = s32[16,8]{1,0:T(8,128)} copy(s32[16,8]{0,1:T(8,128)} %param.8) | data formatting | bytes 1024 | tf_op args[1]
  1.4 55.2 %shard_map.73 = (bf16[256,3,16,128]{3,2,1,0:T(8,128)(2,1)}, f32[16,384]{1,0:T(8,128)}) custom-call(bf16[128,1024]{1,0:T(8,128)(2,1)} %bitcast.3, s32[16,8]{1,0:T(8,128)} %copy.8.flag_ref, bf16[128,128]{1,0:T(8,128)(2,1)} %constant.13.clone.row_ref, bf16[1024,1024]{1,0:T(8,128)(2,1)} %constant.17.hi_hbm, bf16[1024,1024]{1,0:T(8,128)(2,1)} %constant.18.lo_hbm, ...), custom_call_target="tpu_custom_call" | custom-call | tf_op jit(solution)/shard_map/pallas_call | solution.py:269
  56.6 4.1 %copy.10 = bf16[256,16,3,128]{3,1,2,0:T(8,128)(2,1)} copy(bf16[256,16,3,128]{3,1,2,0:T(8,128)(2,1)} %bitcast.2) | data formatting | bytes 6291456
